TPU v7x, 32 devices: a whole 2x2x4 slice. The times are simulated.
32 devices in a mesh: space: 4 (over y, core), ctx: 8 (over z, x).
Axes of the slice: x: 2, y: 2, z: 4, core: 2. Of those that a mesh axis runs over, the one named last changes fastest.
Arguments:
- feats: bfloat16 [4, 8192, 256], P('space', 'ctx'), may hold values from -6 to 6
- face_rows: int32 [4, 2048], P('space', 'ctx'), may hold values from 0 to 1023
- neighbours: int32 [4, 8192, 6], P('space', 'ctx'), may hold values from 0 to 2048
- block_len: int32 [4, 64], P('space'), may hold values from 32 to 128
- dilated: int32 [4, 64, 4], P('space', 'ctx'), may hold values from 0 to 7, as said below
- pick: int32 [4, 8, 8], P('space'), may hold values from 0 to 7
- cpe_weight: bfloat16 [7, 256, 256], replicated, may hold values from -0.125 to 0.125
- cpe_bias: float32 [256], replicated, may hold values from -3 to 3
- ln_gain: float32 [256], replicated, may hold values from 0.1 to 1.9
- ln_bias: float32 [256], replicated, may hold values from -3 to 3
- w_qkv: bfloat16 [256, 768], replicated, may hold values from -11 to 11
- w_out: bfloat16 [256, 256], replicated, may hold values from -3 to 3
Outputs:
- mixed: bfloat16 [4, 8192, 256], P('space', 'ctx')
Inputs may be any that keep to these rules, and one draw needn't show every extreme that they name: `dilated`: among the 32 entries of the blocks of one range, every value 0 to 7 appears.
All inputs are finite; a program needn't handle non-finite values.
Results may differ from a plain program's by a relative error of at most 0.009.
The roundings to bfloat16 on the way count: a program that leaves them out, or rounds other values in their place, can miss the bound.
Values may be sent and summed in bfloat16 or wider, within the bound.
A program may use at most 128 MiB of HBM per device.

v0:
```python
import functools
import math

import jax
import jax.numpy as jnp
from jax import lax
from jax.experimental import pallas as pl
from jax.experimental.pallas import tpu as pltpu
from jax.sharding import PartitionSpec as P

D = 256
HEADS = 8
BLK = 128
EDGE = 128
FACE = 256


MESH = pl.DeviceIdType.MESH


def table_kernel(n_space, n_ctx, rows_ref, own_ref, table_ref, face_ref, send_sem, recv_sem):
    space, ctx = lax.axis_index("space"), lax.axis_index("ctx")
    count = own_ref.shape[0]
    base = count + 2 * EDGE
    sides = (
        (ctx < n_ctx - 1, ctx > 0, (space, ctx + 1)),
        (ctx > 0, ctx < n_ctx - 1, (space, ctx - 1)),
        (space < n_space - 1, space > 0, (space + 1, ctx)),
        (space > 0, space < n_space - 1, (space - 1, ctx)),
    )
    barrier = pltpu.get_barrier_semaphore()
    for there, _, peer in sides:
        @pl.when(there)
        def _():
            pl.semaphore_signal(barrier, inc=1, device_id=peer, device_id_type=MESH)
    pl.semaphore_wait(barrier, sum(there.astype(jnp.int32) for there, _, _ in sides))
    targets = (
        (0, EDGE), (EDGE + count, EDGE), (base, FACE), (base + 2 * FACE, FACE)
    )
    sources = (
        own_ref.at[pl.ds(count - EDGE, EDGE)], own_ref.at[pl.ds(0, EDGE)], face_ref, face_ref
    )
    copies = [
        pltpu.make_async_remote_copy(
            src_ref=sources[i],
            dst_ref=table_ref.at[pl.ds(*targets[i])],
            send_sem=send_sem.at[i],
            recv_sem=recv_sem.at[i],
            device_id=sides[i][2],
            device_id_type=MESH,
        )
        for i in range(4)
    ]
    for i in (0, 1):
        pl.when(sides[i][0])(copies[i].start)
    place = lax.broadcasted_iota(jnp.int32, (FACE, count), 1)
    hot = jnp.where(rows_ref[...] == place, 1.0, 0.0).astype(jnp.bfloat16)
    face = jnp.dot(hot, own_ref[...], preferred_element_type=jnp.float32).astype(jnp.bfloat16)
    face_ref[...] = face
    for i in (2, 3):
        pl.when(sides[i][0])(copies[i].start)
    table_ref[EDGE : EDGE + count, :] = own_ref[...]
    table_ref[base + FACE : base + 2 * FACE, :] = face
    for i in range(4):
        first, width = targets[i]

        @pl.when(jnp.logical_not(sides[i][1]))
        def _():
            table_ref[first : first + width, :] = jnp.zeros((width, D), jnp.bfloat16)
    for i in range(4):
        pl.when(sides[i][0])(copies[i].wait_send)
        pl.when(sides[i][1])(copies[i].wait_recv)


def build_table(rows, own, n_space, n_ctx):
    count, width = own.shape
    vmem = pl.BlockSpec(memory_space=pltpu.VMEM)
    return pl.pallas_call(
        functools.partial(table_kernel, n_space, n_ctx),
        in_specs=[vmem, vmem],
        out_specs=vmem,
        out_shape=jax.ShapeDtypeStruct((count + 2 * EDGE + 3 * FACE, width), own.dtype),
        scratch_shapes=[
            pltpu.VMEM((FACE, width), own.dtype),
            pltpu.SemaphoreType.DMA((4,)),
            pltpu.SemaphoreType.DMA((4,)),
        ],
        compiler_params=pltpu.CompilerParams(
            collective_id=0, has_side_effects=True, vmem_limit_bytes=8 * 2**20
        ),
    )(rows[:, None], own)


def exchange_kernel(n_ctx, out_ref, ends_ref, far_ref, send_sem, recv_sem, local_sem):
    space, ctx = lax.axis_index("space"), lax.axis_index("ctx")
    barrier = pltpu.get_barrier_semaphore()
    for step in range(1, n_ctx):
        peer = lax.rem(ctx + step, n_ctx)
        pl.semaphore_signal(barrier, inc=1, device_id=(space, peer), device_id_type=MESH)
    pl.semaphore_wait(barrier, n_ctx - 1)
    copies = []
    for step in range(1, n_ctx):
        peer = lax.rem(ctx + step, n_ctx)
        copies.append(
            pltpu.make_async_remote_copy(
                src_ref=out_ref.at[peer],
                dst_ref=far_ref.at[ctx],
                send_sem=send_sem.at[step],
                recv_sem=recv_sem.at[step],
                device_id=(space, peer),
                device_id_type=MESH,
            )
        )
    sides = (
        (ctx < n_ctx - 1, ctx > 0, ctx + 1, 1, n_ctx),
        (ctx > 0, ctx < n_ctx - 1, ctx - 1, 0, n_ctx + 1),
    )
    edges = [
        pltpu.make_async_remote_copy(
            src_ref=ends_ref.at[source],
            dst_ref=far_ref.at[slot],
            send_sem=send_sem.at[slot],
            recv_sem=recv_sem.at[slot],
            device_id=(space, peer),
            device_id_type=MESH,
        )
        for _, _, peer, source, slot in sides
    ]
    order = sorted(range(1, n_ctx), key=lambda step: abs(step - n_ctx // 2))
    for step in order:
        copies[step - 1].start()
    for side, edge in zip(sides, edges):
        pl.when(side[0])(edge.start)
    own = pltpu.make_async_copy(out_ref.at[ctx], far_ref.at[ctx], local_sem)
    own.start()
    for side in sides:
        @pl.when(jnp.logical_not(side[1]))
        def _():
            far_ref[side[4]] = jnp.zeros(far_ref.shape[1:], jnp.bfloat16)
    own.wait()
    for copy in copies:
        copy.wait()
    for side, edge in zip(sides, edges):
        pl.when(side[0])(edge.wait_send)
        pl.when(side[1])(edge.wait_recv)


def exchange(outgoing, ends, n_ctx):
    vmem = pl.BlockSpec(memory_space=pltpu.VMEM)
    return pl.pallas_call(
        functools.partial(exchange_kernel, n_ctx),
        in_specs=[vmem, vmem],
        out_specs=vmem,
        out_shape=jax.ShapeDtypeStruct((n_ctx + 2,) + outgoing.shape[1:], outgoing.dtype),
        scratch_shapes=[
            pltpu.SemaphoreType.DMA((n_ctx + 2,)),
            pltpu.SemaphoreType.DMA((n_ctx + 2,)),
            pltpu.SemaphoreType.DMA,
        ],
        compiler_params=pltpu.CompilerParams(
            collective_id=1, has_side_effects=True, vmem_limit_bytes=8 * 2**20
        ),
    )(outgoing, ends)


ROWS = 1024


def encode_kernel(
    pick_ref, ids_ref, table_ref, weight_ref, bias_ref, gain_ref, shift_ref, qkv_ref,
    hidden_ref, query_ref, kv_ref, outgoing_ref, ends_ref, normed_ref,
):
    rows = ids_ref.shape[0]
    count = table_ref.shape[0]
    step = pl.program_id(0)
    own = table_ref[pl.ds(pl.multiple_of(EDGE + step * rows, EDGE), rows), :]
    conv = jnp.dot(own, weight_ref[0], preferred_element_type=jnp.float32)
    lane = lax.broadcasted_iota(jnp.int32, (rows, 128), 1)
    ids = ids_ref[...]
    for offset in range(6):
        column = jnp.broadcast_to(ids[:, offset : offset + 1], (rows, 128))
        low = column & 127
        high = (column >> 7).astype(jnp.float32).astype(jnp.bfloat16)
        hot = jnp.where(low == lane, 1.0, 0.0).astype(jnp.bfloat16)
        zero = jnp.zeros_like(hot)
        chosen = jnp.concatenate(
            [jnp.where(high == jnp.bfloat16(part), hot, zero) for part in range(count // 128)], 1
        )
        picked = jnp.dot(chosen, table_ref[...], preferred_element_type=jnp.float32)
        conv = conv + jnp.dot(
            picked.astype(jnp.bfloat16), weight_ref[offset + 1], preferred_element_type=jnp.float32
        )
    hidden = own.astype(jnp.float32) + conv + bias_ref[...]
    hidden_ref[...] = hidden
    center = hidden - jnp.mean(hidden, axis=-1, keepdims=True)
    variance = jnp.mean(center * center, axis=-1, keepdims=True)
    normed = (center * lax.rsqrt(variance + 1e-05) * gain_ref[...] + shift_ref[...]).astype(jnp.bfloat16)
    projected = jnp.dot(normed, qkv_ref[...], preferred_element_type=jnp.float32).astype(jnp.bfloat16)
    query_ref[...] = projected[:, :D]
    kv_ref[...] = projected[:, D:]
    normed_ref[pl.ds(pl.multiple_of(step * rows, rows), rows), :] = normed

    @pl.when(step == pl.num_programs(0) - 1)
    def _():
        ends_ref[0] = normed_ref[:BLK, :]
        ends_ref[1] = normed_ref[normed_ref.shape[0] - BLK :, :]
        for peer in range(outgoing_ref.shape[0]):
            first = pl.multiple_of(pick_ref[lax.axis_index("ctx"), peer] * BLK, BLK)
            outgoing_ref[peer] = normed_ref[pl.ds(first, BLK), :]


def encode(pick, ids, table, weight, bias, gain, shift, w_qkv):
    count, width = ids.shape[0], table.shape[1]
    whole = lambda shape: pl.BlockSpec(shape, lambda i, *_: (0,) * len(shape))
    tile = lambda cols: pl.BlockSpec((ROWS, cols), lambda i, *_: (i, 0))
    peers = pick.shape[0]
    return pl.pallas_call(
        encode_kernel,
        grid_spec=pltpu.PrefetchScalarGridSpec(
            num_scalar_prefetch=1,
            grid=(count // ROWS,),
            in_specs=[
                tile(6), whole(table.shape), whole(weight.shape),
                whole((1, width)), whole((1, width)), whole((1, width)), whole(w_qkv.shape),
            ],
            out_specs=[
                tile(width), tile(width), tile(2 * width),
                whole((peers, BLK, width)), whole((2, BLK, width)),
            ],
            scratch_shapes=[pltpu.VMEM((count, width), jnp.bfloat16)],
        ),
        out_shape=[
            pltpu.HBM((count, width), jnp.float32),
            jax.ShapeDtypeStruct((count, width), jnp.bfloat16),
            jax.ShapeDtypeStruct((count, 2 * width), jnp.bfloat16),
            jax.ShapeDtypeStruct((peers, BLK, width), jnp.bfloat16),
            jax.ShapeDtypeStruct((2, BLK, width), jnp.bfloat16),
        ],
        compiler_params=pltpu.CompilerParams(vmem_limit_bytes=20 * 2**20),
    )(pick, ids, table, weight, bias[None], gain[None], shift[None], w_qkv)


HALF = 128
CHUNK = 4
AHEAD = 1


def attend_kernel(
    slots_ref, lens_ref, pick_ref, query_ref, near_ref, far_ref, qkv_ref, hidden_ref, out_w_ref,
    out_ref, far_kv_ref, window_ref, keys_ref, values_ref,
):
    blk = pl.program_id(0)
    peers = pick_ref.shape[0]
    count = near_ref.shape[0]
    blocks = count // BLK
    ctx = lax.axis_index("ctx")

    @pl.when(blk == 0)
    def _():
        kv_weight = qkv_ref[:, D:]
        for peer in range(peers):
            far_kv_ref[peer * BLK : (peer + 1) * BLK, :] = jnp.dot(
                far_ref[peer], kv_weight, preferred_element_type=jnp.float32
            ).astype(jnp.bfloat16)
        window_ref[BLK : BLK + count, :] = near_ref[...]
        for side, first in ((peers, 0), (peers + 1, BLK + count)):
            window_ref[first : first + BLK, :] = jnp.dot(
                far_ref[side], kv_weight, preferred_element_type=jnp.float32
            ).astype(jnp.bfloat16)

        values_ref[:, :, HALF:] = jnp.ones((D // HALF, 7 * BLK, HALF), jnp.bfloat16)

    row = lax.broadcasted_iota(jnp.int32, (BLK, HALF), 0)
    lane = lax.broadcasted_iota(jnp.int32, (BLK, HALF), 1)
    for part in range(7):
        if part < 3:
            block = ctx * blocks + blk + part - 1
            inside = jnp.logical_and(block >= 0, block < peers * blocks)
            valid = jnp.where(inside, lens_ref[jnp.clip(block, 0, peers * blocks - 1)], 0)
            source = window_ref.at[pl.ds(pl.multiple_of((blk + part) * BLK, BLK), BLK)]
        else:
            slot = slots_ref[blk, part - 3]
            valid = lens_ref[slot * blocks + pick_ref[slot, ctx]]
            source = far_kv_ref.at[pl.ds(pl.multiple_of(slot * BLK, BLK), BLK)]
        masked = jnp.where(jnp.logical_and(row >= valid, lane == 0), -1e30, 0.0).astype(jnp.bfloat16)
        first = part * BLK
        for group in range(D // HALF):
            keys_ref[group, first : first + BLK, :HALF] = source[:, group * HALF : (group + 1) * HALF]
            keys_ref[group, first : first + BLK, HALF:] = masked
            values_ref[group, first : first + BLK, :HALF] = source[
                :, D + group * HALF : D + (group + 1) * HALF
            ]
    head_dim = D // HEADS
    head_of = lane // head_dim
    heads = HALF // head_dim
    adds_mask = jnp.where(lane == 0, 1.0, 0.0).astype(jnp.bfloat16)
    scale = math.log2(math.e) / math.sqrt(head_dim)
    chunks = [(group, first) for group in range(D // HALF) for first in range(0, heads, CHUNK)]

    def score(group, first):
        query = query_ref[:, group * HALF : (group + 1) * HALF]
        stacked = jnp.concatenate(
            [
                jnp.concatenate([jnp.where(head_of == head, query, jnp.zeros_like(query)), adds_mask], 1)
                for head in range(first, first + CHUNK)
            ],
            0,
        )
        return lax.dot_general(
            stacked, keys_ref[group], (((1,), (1,)), ((), ())), preferred_element_type=jnp.float32
        )

    halves = [jnp.zeros((BLK, HALF), jnp.float32) for _ in range(D // HALF)]
    ahead = [score(*chunk) for chunk in chunks[:AHEAD]]
    for turn, (group, first) in enumerate(chunks):
        if turn + AHEAD < len(chunks):
            ahead.append(score(*chunks[turn + AHEAD]))
        scores = ahead[turn]
        peak = jnp.max(scores, axis=-1, keepdims=True)
        weights = jnp.exp2((scores - peak) * scale).astype(jnp.bfloat16)
        mixed = jnp.dot(weights, values_ref[group], preferred_element_type=jnp.float32)
        mixed = mixed[:, :HALF] / mixed[:, HALF:]
        for head in range(CHUNK):
            halves[group] = jnp.where(
                head_of == first + head, mixed[head * BLK : (head + 1) * BLK], halves[group]
            )
    attended = jnp.concatenate(halves, 1)
    out = hidden_ref[...] + jnp.dot(
        attended.astype(jnp.bfloat16), out_w_ref[...], preferred_element_type=jnp.float32
    )
    out_ref[...] = out.astype(jnp.bfloat16)


def attend(slots, lens, pick, queries, near, far, w_qkv, hidden, w_out):
    count, width = queries.shape
    whole = lambda shape: pl.BlockSpec(shape, lambda i, *_: (0,) * len(shape))
    tile = pl.BlockSpec((BLK, width), lambda i, *_: (i, 0))
    return pl.pallas_call(
        attend_kernel,
        grid_spec=pltpu.PrefetchScalarGridSpec(
            num_scalar_prefetch=3,
            grid=(count // BLK,),
            in_specs=[
                tile, whole(near.shape), whole(far.shape), whole(w_qkv.shape), tile, whole(w_out.shape)
            ],
            out_specs=tile,
            scratch_shapes=[
                pltpu.VMEM((pick.shape[0] * BLK, 2 * width), jnp.bfloat16),
                pltpu.VMEM((count + 2 * BLK, 2 * width), jnp.bfloat16),
                pltpu.VMEM((width // HALF, 7 * BLK, 2 * HALF), jnp.bfloat16),
                pltpu.VMEM((width // HALF, 7 * BLK, 2 * HALF), jnp.bfloat16),
            ],
        ),
        out_shape=jax.ShapeDtypeStruct((count, width), jnp.bfloat16),
        compiler_params=pltpu.CompilerParams(vmem_limit_bytes=32 * 2**20),
    )(slots, lens, pick, queries, near, far, w_qkv, hidden, w_out)


def on_device(
    feats,
    face_rows,
    neighbours,
    block_len,
    dilated,
    pick,
    cpe_weight,
    cpe_bias,
    ln_gain,
    ln_bias,
    w_qkv,
    w_out,
):
    voxels = feats[0]
    n_space, n_ctx = lax.axis_size("space"), lax.axis_size("ctx")
    table = build_table(face_rows[0], voxels, n_space, n_ctx)
    hidden, queries, near, outgoing, ends = encode(
        pick[0], neighbours[0], table, cpe_weight, cpe_bias, ln_gain, ln_bias, w_qkv
    )
    hidden = pltpu.with_memory_space_constraint(hidden, pltpu.HBM)
    far = exchange(outgoing, ends, n_ctx)
    return attend(dilated[0], block_len[0], pick[0], queries, near, far, w_qkv, hidden, w_out)[None]


def solution(mesh):
    placed = (
        P("space", "ctx", None),
        P("space", "ctx"),
        P("space", "ctx", None),
        P("space", None),
        P("space", "ctx", None),
        P("space", None, None),
        P(),
        P(),
        P(),
        P(),
        P(),
        P(),
    )
    return jax.shard_map(
        on_device, mesh=mesh, in_specs=placed, out_specs=P("space", "ctx", None), check_vma=False
    )
```

profile of v0, /device:TPU:16, one launch (start us, length us, event | category | flops | bytes accessed | tf_op | source)
XLA Modules:
  0.0 58.8 jit_solution(9347330096440421822)
XLA Ops:
  0.0 0.0 copy-start.11
  0.0 0.7 %copy-done.11 = s32[1,256]{1,0:T(1,128)S(1)} copy-done((s32[1,256]{1,0:T(1,128)S(1)}, s32[1,256]{1,0:T(1,128)}, u32[]{:S(2)}) %copy-start.11) | copy-done | bytes 1048
  0.7 0.1 copy.16.rows_ref
  0.8 0.0 copy-start.2
  0.8 1.0 %copy-done.2 = bf16[1,1024,256]{2,1,0:T(8,128)(2,1)S(1)} copy-done((bf16[1,1024,256]{2,1,0:T(8,128)(2,1)S(1)}, bf16[1,1024,256]{2,1,0:T(8,128)(2,1)}, u32[]{:S(2)}) %copy-start.2) | copy-done | bytes 524312
  1.9 0.0 copy-start.9
  1.9 6.7 %shard_map.118.table_ref = bf16[2048,256]{1,0:T(8,128)(2,1)S(1)} custom-call(s32[256,1]{1,0:T(8,128)S(1)} %copy.16.rows_ref, bf16[1024,256]{1,0:T(8,128)(2,1)S(1)} %bitcast.11), custom_call_target="tpu_custom_call" | custom-call | tf_op jit(solution)/shard_map/pallas_call | solution.py:78
  8.6 0.0 copy-done.9
  8.6 0.0 copy-start
  8.6 0.0 copy-start.6
  8.7 0.0 copy-start.7
  8.7 0.2 copy.15
  8.9 0.0 copy-start.4
  8.9 0.0 copy-start.5
  8.9 0.7 %copy-done = bf16[256,768]{1,0:T(8,128)(2,1)S(1)} copy-done((bf16[256,768]{1,0:T(8,128)(2,1)S(1)}, bf16[256,768]{1,0:T(8,128)(2,1)}, u32[]{:S(2)}) %copy-start) | copy-done | bytes 393240
  9.6 0.0 copy-done.6
  9.6 0.0 copy-done.7
  9.6 0.0 copy-done.4
  9.6 0.0 copy-done.5
  9.6 0.0 copy-start.1
  9.7 1.2 %copy-done.1 = bf16[7,256,256]{2,1,0:T(8,128)(2,1)S(1)} copy-done((bf16[7,256,256]{2,1,0:T(8,128)(2,1)S(1)}, bf16[7,256,256]{2,1,0:T(8,128)(2,1)}, u32[]{:S(2)}) %copy-start.1) | copy-done | bytes 917528
  10.8 12.3 %shard_map.119 = (f32[1024,256]{1,0:T(8,128)}, bf16[1024,256]{1,0:T(8,128)(2,1)S(1)}, bf16[1024,512]{1,0:T(8,128)(2,1)S(1)}, bf16[8,128,256]{2,1,0:T(8,128)(2,1)S(1)}, bf16[2,128,256]{2,1,0:T(8,128)(2,1)S(1)}) custom-call(s32[8,8]{1,0:T(8,128)S(1)} %bitcast.12, s32[1024,6]{1,0:T(8,128)S(1)} %bitcast.10, bf16[2048,256]{1,0:T(8,128)(2,1)S(1)} %shard_map.118.table_ref, ...), custom_call_target="tpu_custom_call" | custom-call | tf_op jit(solution)/shard_map/pallas_call | solution.py:217
  23.2 0.0 copy-start.3
  23.2 16.9 %shard_map.120.far_ref = bf16[10,128,256]{2,1,0:T(8,128)(2,1)S(1)} custom-call(bf16[8,128,256]{2,1,0:T(8,128)(2,1)S(1)} %get-tuple-element.12.out_ref, bf16[2,128,256]{2,1,0:T(8,128)(2,1)S(1)} %get-tuple-element.13.ends_ref), custom_call_target="tpu_custom_call" | custom-call | tf_op jit(solution)/shard_map/pallas_call | solution.py:150
  40.1 0.0 copy-start.10
  40.1 0.7 %copy-done.10 = s32[1,8,4]{1,2,0:T(4,128)S(1)} copy-done((s32[1,8,4]{1,2,0:T(4,128)S(1)}, s32[1,8,4]{1,2,0:T(4,128)}, u32[]{:S(2)}) %copy-start.10) | copy-done | bytes 152
  40.8 0.1 copy.17.slots_ref
  40.8 0.0 copy-start.8
  40.8 0.0 copy-done.3
  40.8 0.7 %copy-done.8 = s32[1,64]{1,0:T(1,128)S(1)} copy-done((s32[1,64]{1,0:T(1,128)S(1)}, s32[1,64]{1,0:T(1,128)}, u32[]{:S(2)}) %copy-start.8) | copy-done | bytes 280
  41.5 17.3 %shard_map.121 = bf16[1024,256]{1,0:T(8,128)(2,1)} custom-call(s32[8,4]{1,0:T(8,128)S(1)} %copy.17.slots_ref, s32[64]{0:T(128)S(1)} %bitcast.17, s32[8,8]{1,0:T(8,128)S(1)} %bitcast.13, bf16[1024,256]{1,0:T(8,128)(2,1)S(1)} %get-tuple-element.10.query_ref, bf16[1024,512]{1,0:T(8,128)(2,1)S(1)} %get-tuple-element.11.near_ref, ...), custom_call_target="tpu_custom_call" | custom-call | tf_op jit(solution)/shard_map/pallas_call | solution.py:338
Async XLA Ops:
  0.0 0.7 %copy-start.11 = (s32[1,256]{1,0:T(1,128)S(1)}, s32[1,256]{1,0:T(1,128)}, u32[]{:S(2)}) copy-start(s32[1,256]{1,0:T(1,128)} %param.13) | copy-start | bytes 3076
  0.8 1.0 %copy-start.2 = (bf16[1,1024,256]{2,1,0:T(8,128)(2,1)S(1)}, bf16[1,1024,256]{2,1,0:T(8,128)(2,1)}, u32[]{:S(2)}) copy-start(bf16[1,1024,256]{2,1,0:T(8,128)(2,1)} %param.12) | copy-start | bytes 1572868
  1.9 6.8 %copy-start.9 = (s32[1,1024,6]{1,0,2:T(1,128)S(1)}, s32[1,1024,6]{1,0,2:T(1,128)}, u32[]{:S(2)}) copy-start(s32[1,1024,6]{1,0,2:T(1,128)} %param.14) | copy-start | bytes 73732
  8.6 1.0 %copy-start = (bf16[256,768]{1,0:T(8,128)(2,1)S(1)}, bf16[256,768]{1,0:T(8,128)(2,1)}, u32[]{:S(2)}) copy-start(bf16[256,768]{1,0:T(8,128)(2,1)} %qkv_ref.3) | copy-start | bytes 1179652
  8.6 1.0 %copy-start.6 = (f32[256]{0:T(256)S(1)}, f32[256]{0:T(256)}, u32[]{:S(2)}) copy-start(f32[256]{0:T(256)} %param.20) | copy-start | bytes 3076
  8.7 1.0 %copy-start.7 = (f32[256]{0:T(256)S(1)}, f32[256]{0:T(256)}, u32[]{:S(2)}) copy-start(f32[256]{0:T(256)} %param.21) | copy-start | bytes 3076
  8.9 0.7 %copy-start.4 = (s32[1,8,8]{2,1,0:T(8,128)S(1)}, s32[1,8,8]{2,1,0:T(8,128)}, u32[]{:S(2)}) copy-start(s32[1,8,8]{2,1,0:T(8,128)} %param.17) | copy-start | bytes 772
  8.9 0.7 %copy-start.5 = (f32[256]{0:T(256)S(1)}, f32[256]{0:T(256)}, u32[]{:S(2)}) copy-start(f32[256]{0:T(256)} %param.19) | copy-start | bytes 3076
  9.6 1.2 %copy-start.1 = (bf16[7,256,256]{2,1,0:T(8,128)(2,1)S(1)}, bf16[7,256,256]{2,1,0:T(8,128)(2,1)}, u32[]{:S(2)}) copy-start(bf16[7,256,256]{2,1,0:T(8,128)(2,1)} %weight_ref.1) | copy-start | bytes 2752516
  23.2 17.7 %copy-start.3 = (bf16[256,256]{1,0:T(8,128)(2,1)S(1)}, bf16[256,256]{1,0:T(8,128)(2,1)}, u32[]{:S(2)}) copy-start(bf16[256,256]{1,0:T(8,128)(2,1)} %out_w_ref.1) | copy-start | bytes 393220
  40.1 0.7 %copy-start.10 = (s32[1,8,4]{1,2,0:T(4,128)S(1)}, s32[1,8,4]{1,2,0:T(4,128)}, u32[]{:S(2)}) copy-start(s32[1,8,4]{1,2,0:T(4,128)} %param.16) | copy-start | bytes 388
  40.8 0.7 %copy-start.8 = (s32[1,64]{1,0:T(1,128)S(1)}, s32[1,64]{1,0:T(1,128)}, u32[]{:S(2)}) copy-start(s32[1,64]{1,0:T(1,128)} %param.15) | copy-start | bytes 772
where the time goes:
time: 59.1 us; the launch traced here: 58.8 us
  Pallas kernels  53.3 us (90%)
  local copies, waits for them, and re-layouts  5.4 us (9%)
    pallas_call x1, Pallas kernels, attend(): pl.pallas_call(attend_kernel, grid_spec=pltpu.PrefetchScalarGridSpec(num_...  17.3 us
    pallas_call x1, Pallas kernels, exchange(): pl.pallas_call(functools.partial(exchange_kernel, n_ctx), in_specs=[vmem,...  16.9 us
    pallas_call x1, Pallas kernels, encode(): pl.pallas_call(encode_kernel, grid_spec=pltpu.PrefetchScalarGridSpec(num_...  12.3 us
    pallas_call x1, Pallas kernels, build_table(): pl.pallas_call(functools.partial(table_kernel, n_space, n_ctx), in_specs=...  6.74 us
    unnamed x25, local copies, waits for them, and re-layouts  5.19 us

commit v1 on v0

v1 whole, which is shorter than its diff:
```python
import functools
import math

import jax
import jax.numpy as jnp
from jax import lax
from jax.experimental import pallas as pl
from jax.experimental.pallas import tpu as pltpu
from jax.sharding import PartitionSpec as P

D = 256
HEADS = 8
BLK = 128
EDGE = 128
FACE = 256
HALF = 128
OFFSETS = 6

MESH = pl.DeviceIdType.MESH
BF16 = jnp.bfloat16
F32 = jnp.float32

LOCAL_PARTS = tuple(range(1, 9)) + (12, 13)
SENT_PARTS = (0, 9, 10, 11, 14, 15)
EARLY = 4


def zero_like(value):
    return jnp.zeros_like(value)


def body(
    n_space, n_ctx,
    feats, face_rows, neighbours, block_len, dilated, pick, cpe_weight, cpe_bias, ln_gain, ln_bias, w_qkv, w_out,
    out_ref,
    table, rows_v, ids_v, weight_v, bias_v, gain_v, shift_v, qkv_v, outw_v,
    lens_s, slots_s, pick_s, pos_s, perm_s,
    early, hidden_s, query_s, normed_s, key_s, value_s, ones_s, outgoing, ends, far,
    near_peak, near_sum, near_den,
    load_sem, table_send, table_recv, send_sem, recv_sem,
):
    space, ctx = lax.axis_index("space"), lax.axis_index("ctx")
    blocks = feats.shape[0]
    count = blocks * BLK
    local = count + FACE

    barrier = pltpu.get_barrier_semaphore()

    def ctx_peer(j):
        half = n_ctx // 2
        mine = ctx // half
        other = (1 - mine) * half + lax.rem(ctx + j, half)
        same = mine * half + lax.rem(ctx + j + 1, half)
        return jnp.where(j < half, other, same)

    for j in range(n_ctx - 1):
        pl.semaphore_signal(barrier, inc=1, device_id=(space, ctx_peer(j)), device_id_type=MESH)
    sides = (
        (ctx < n_ctx - 1, ctx > 0, (space, ctx + 1)),
        (ctx > 0, ctx < n_ctx - 1, (space, ctx - 1)),
        (space < n_space - 1, space > 0, (space + 1, ctx)),
        (space > 0, space < n_space - 1, (space - 1, ctx)),
    )
    for there, _, peer in sides[2:]:
        @pl.when(there)
        def _():
            pl.semaphore_signal(barrier, inc=1, device_id=peer, device_id_type=MESH)

    loads = [
        pltpu.make_async_copy(source, target, load_sem.at[i])
        for i, (source, target) in enumerate((
            (feats, table.at[pl.ds(0, blocks)]),
            (face_rows, rows_v),
            (pick, pick_s),
            (neighbours, ids_v),
            (block_len, lens_s),
            (dilated, slots_s),
            (cpe_weight, weight_v),
            (cpe_bias, bias_v),
            (ln_gain, gain_v),
            (ln_bias, shift_v),
            (w_qkv, qkv_v),
            (w_out, outw_v),
        ))
    ]
    for load in loads:
        load.start()

    lane = lax.broadcasted_iota(jnp.int32, (BLK, HALF), 1)
    row = lax.broadcasted_iota(jnp.int32, (BLK, 1), 0)

    def split_ids(columns):
        spread = jnp.concatenate([jnp.broadcast_to(ids, (BLK, BLK)).T for ids in columns], 0)
        lanes = lax.broadcasted_iota(jnp.int32, spread.shape, 1)
        hot = jnp.where((spread & (BLK - 1)) == lanes, 1.0, 0.0).astype(BF16)
        return hot, (spread >> 7).astype(F32).astype(BF16)

    def choose(hot, high, parts):
        return jnp.concatenate([jnp.where(high == BF16(part), hot, zero_like(hot)) for part in parts], 1)

    loads[0].wait()
    loads[1].wait()
    hot, high = split_ids([rows_v[:, i * BLK : (i + 1) * BLK] for i in range(FACE // BLK)])
    table[blocks : local // BLK] = jnp.dot(
        choose(hot, high, range(blocks)), table[:blocks].reshape(count, D), preferred_element_type=F32
    ).astype(BF16).reshape(FACE // BLK, BLK, D)

    pl.semaphore_wait(
        barrier, n_ctx - 1 + sides[2][0].astype(jnp.int32) + sides[3][0].astype(jnp.int32)
    )
    pieces = (
        (count - EDGE, local, EDGE),
        (0, local + EDGE, EDGE),
        (count, local + 2 * EDGE, FACE),
        (count, local + 2 * EDGE + FACE, FACE),
    )
    copies = [
        pltpu.make_async_remote_copy(
            src_ref=table.at[pl.ds(source // BLK, size // BLK)],
            dst_ref=table.at[pl.ds(target // BLK, size // BLK)],
            send_sem=table_send.at[i],
            recv_sem=table_recv.at[i],
            device_id=sides[i][2],
            device_id_type=MESH,
        )
        for i, (source, target, size) in enumerate(pieces)
    ]
    for i in (2, 3, 0, 1):
        pl.when(sides[i][0])(copies[i].start)
    for i, (_, target, size) in enumerate(pieces):
        @pl.when(jnp.logical_not(sides[i][1]))
        def _():
            table[target // BLK : (target + size) // BLK] = jnp.zeros((size // BLK, BLK, D), BF16)

    loads[2].wait()
    wanted = [pick_s[0, ctx, ctx_peer(j)] for j in range(n_ctx)]
    need = [jnp.int32(n_ctx + b) for b in range(blocks)]
    for j in reversed(range(n_ctx)):
        need = [jnp.where(wanted[j] == b, j, need[b]) for b in range(blocks)]
    position = [
        sum((need[a] < need[b]).astype(jnp.int32) for a in range(blocks) if a != b) for b in range(blocks)
    ]
    for b in range(blocks):
        pos_s[b] = position[b]
    for j in range(blocks):
        perm_s[j] = sum(jnp.where(position[b] == j, b, 0) for b in range(blocks))

    for load in loads[3:]:
        load.wait()

    def block_at(ref, index):
        return ref[index]

    def table_rows(first, last):
        return table[first // BLK : last // BLK].reshape(last - first, D)

    def step_ids(j):
        at = perm_s[j]
        return split_ids([ids_v[o, at] for o in range(OFFSETS)])

    def pick_early(j, carry):
        hot, high = step_ids(j)
        early[j] = jnp.dot(
            choose(hot, high, LOCAL_PARTS), table_rows(0, local), preferred_element_type=F32
        ).astype(BF16)
        return carry

    lax.fori_loop(0, EARLY, pick_early, 0)

    for i in range(4):
        pl.when(sides[i][0])(copies[i].wait_send)
        pl.when(sides[i][1])(copies[i].wait_recv)

    def keep(index, keys, values, valid, spare):
        inside = row < valid
        key_s[index] = jnp.where(inside, keys, spare).astype(BF16)
        value_s[index] = jnp.where(inside, values, 0.0).astype(BF16)
        ones_s[index] = jnp.where(jnp.broadcast_to(inside, (BLK, HALF)), 1.0, 0.0).astype(BF16)

    def send(j):
        return pltpu.make_async_remote_copy(
            src_ref=outgoing.at[j],
            dst_ref=far.at[ctx],
            send_sem=send_sem.at[j],
            recv_sem=recv_sem.at[j],
            device_id=(space, ctx_peer(j)),
            device_id_type=MESH,
        )

    def start_send(j):
        outgoing[j] = block_at(normed_s, pos_s[pick_s[0, ctx, ctx_peer(j)]])
        send(j).start()

    def finish(j, picked):
        block = perm_s[j]
        own = block_at(table, block)
        taps = jnp.concatenate([own] + [picked[o * BLK : (o + 1) * BLK] for o in range(OFFSETS)], 1)
        conv = jnp.dot(taps, weight_v[...], preferred_element_type=F32)
        hidden = own.astype(F32) + conv + bias_v[...]
        hidden_s[j] = hidden
        center = hidden - jnp.mean(hidden, axis=-1, keepdims=True)
        variance = jnp.mean(center * center, axis=-1, keepdims=True)
        normed = (center * lax.rsqrt(variance + 1e-05) * gain_v[...] + shift_v[...]).astype(BF16)
        normed_s[j] = normed
        projected = jnp.dot(normed, qkv_v[...], preferred_element_type=F32)
        query_s[j] = projected[:, :D].astype(BF16)
        keys = projected[:, D : 2 * D]
        keep(j, keys, projected[:, 2 * D :], lens_s[0, ctx * blocks + block], keys[:1])

        @pl.when(j < n_ctx - 1)
        def _():
            start_send(j)

    def finish_early(j, carry):
        hot, high = step_ids(j)
        sent = jnp.dot(choose(hot, high, SENT_PARTS), table_rows(local, table.shape[0] * BLK), preferred_element_type=F32)
        mine = early[j]
        finish(j, (sent + mine.astype(F32)).astype(BF16))
        return carry

    def finish_late(j, carry):
        hot, high = step_ids(j)
        picked = jnp.dot(choose(hot, high, LOCAL_PARTS + SENT_PARTS), table_rows(0, table.shape[0] * BLK), preferred_element_type=F32)
        finish(j, picked.astype(BF16))
        return carry

    lax.fori_loop(0, EARLY, finish_early, 0)
    lax.fori_loop(EARLY, blocks, finish_late, 0)

    ends[0] = block_at(normed_s, pos_s[0])
    ends[1] = block_at(normed_s, pos_s[blocks - 1])
    edges = [
        pltpu.make_async_remote_copy(
            src_ref=ends.at[source],
            dst_ref=far.at[slot],
            send_sem=send_sem.at[slot],
            recv_sem=recv_sem.at[slot],
            device_id=(space, peer),
            device_id_type=MESH,
        )
        for peer, source, slot in ((ctx + 1, 1, n_ctx), (ctx - 1, 0, n_ctx + 1))
    ]
    for side, edge in zip(sides[:2], edges):
        pl.when(side[0])(edge.start)
    if n_ctx - 1 > blocks:
        lax.fori_loop(blocks, n_ctx - 1, lambda j, carry: (start_send(j), carry)[1], 0)
    far[ctx] = block_at(normed_s, pos_s[pick_s[0, ctx, ctx]])
    for i, side in enumerate(sides[:2]):
        @pl.when(jnp.logical_not(side[1]))
        def _():
            far[n_ctx + i] = jnp.zeros((BLK, D), BF16)

    head_dim = D // HEADS
    heads = HALF // head_dim
    head_of = lane // head_dim
    scale = math.log2(math.e) / math.sqrt(head_dim)
    groups = D // HALF

    def spread(stacked):
        result = None
        for head in range(heads):
            part = stacked[head * BLK : (head + 1) * BLK]
            part = jnp.broadcast_to(part, (BLK, HALF))
            result = part if result is None else jnp.where(head_of == head, part, result)
        return result

    def attend(query, sources):
        def stack(ref, group):
            cols = slice(group * HALF, (group + 1) * HALF)
            return jnp.concatenate([ref[index, :, cols] for index in sources], 0)

        def score(group):
            part = query[:, group * HALF : (group + 1) * HALF]
            stacked = jnp.concatenate(
                [jnp.where(head_of == head, part, zero_like(part)) for head in range(heads)], 0
            )
            return lax.dot_general(
                stacked, stack(key_s, group), (((1,), (1,)), ((), ())), preferred_element_type=F32
            )

        ones = jnp.concatenate([block_at(ones_s, index) for index in sources], 0)
        results = []
        scores = [score(group) for group in range(groups)]
        for group in range(groups):
            peak = jnp.max(scores[group], axis=-1, keepdims=True)
            weights = jnp.exp2((scores[group] - peak) * scale).astype(BF16)
            mixed = jnp.dot(
                weights, jnp.concatenate([stack(value_s, group), ones], 1), preferred_element_type=F32
            )
            results.append((peak, mixed[:, :HALF], mixed[:, HALF:]))
        return results

    def near_blocks(b):
        return [pos_s[b - 1], pos_s[b], pos_s[b + 1]]

    def near(i, carry):
        b = i + 1
        at = pos_s[b]
        for group, (peak, total, den) in enumerate(attend(block_at(query_s, at), near_blocks(b))):
            cols = slice(group * HALF, (group + 1) * HALF)
            near_peak[i, :, cols] = spread(peak)
            near_sum[i, :, cols] = spread(total)
            near_den[i, :, cols] = spread(den)
        return carry

    lax.fori_loop(0, blocks - 2, near, 0)

    for j in range(n_ctx - 1):
        send(j).wait()
    for side, edge in zip(sides[:2], edges):
        pl.when(side[0])(edge.wait_send)
        pl.when(side[1])(edge.wait_recv)

    left, right = blocks + n_ctx, blocks + n_ctx + 1

    def project(s, valid, spare):
        both = jnp.dot(far[s], qkv_v[:, D:], preferred_element_type=F32)
        keys = both[:, :D]
        keep(blocks + s, keys, both[:, D:], valid, keys[:1] if spare is None else spare)

    def project_far(s, carry):
        project(s, lens_s[0, s * blocks + pick_s[0, s, ctx]], None)
        return carry

    lax.fori_loop(0, n_ctx, project_far, 0)
    for s, there, at, inner in (
        (n_ctx, ctx > 0, ctx * blocks - 1, 0),
        (n_ctx + 1, ctx < n_ctx - 1, (ctx + 1) * blocks, blocks - 1),
    ):
        valid = jnp.where(there, lens_s[0, jnp.where(there, at, 0)], 0)
        project(s, valid, block_at(key_s, pos_s[inner])[:1].astype(F32))

    def far_blocks(b):
        return [blocks + slots_s[0, k, b] for k in range(slots_s.shape[1])]

    def write(b, at, attended):
        out_ref[b] = (
            block_at(hidden_s, at)
            + jnp.dot(jnp.concatenate(attended, 1).astype(BF16), outw_v[...], preferred_element_type=F32)
        ).astype(BF16)

    def far_inner(i, carry):
        b = i + 1
        at = pos_s[b]
        attended = []
        for group, (peak, total, den) in enumerate(attend(block_at(query_s, at), far_blocks(b))):
            cols = slice(group * HALF, (group + 1) * HALF)
            peak, other = spread(peak), near_peak[i, :, cols]
            top = jnp.maximum(peak, other)
            mine, theirs = jnp.exp2((peak - top) * scale), jnp.exp2((other - top) * scale)
            attended.append(
                (spread(total) * mine + near_sum[i, :, cols] * theirs)
                / (spread(den) * mine + near_den[i, :, cols] * theirs)
            )
        write(b, at, attended)
        return carry

    lax.fori_loop(0, blocks - 2, far_inner, 0)

    def whole(i, carry):
        b = i * (blocks - 1)
        at = pos_s[b]
        before = jnp.where(i == 0, left, pos_s[jnp.maximum(b - 1, 0)])
        after = jnp.where(i == 0, pos_s[jnp.minimum(b + 1, blocks - 1)], right)
        results = attend(block_at(query_s, at), [before, at, after] + far_blocks(b))
        write(b, at, [spread(total) / spread(den) for _, total, den in results])
        return carry

    lax.fori_loop(0, 2, whole, 0)


def on_device(
    feats,
    face_rows,
    neighbours,
    block_len,
    dilated,
    pick,
    cpe_weight,
    cpe_bias,
    ln_gain,
    ln_bias,
    w_qkv,
    w_out,
):
    n_space, n_ctx = lax.axis_size("space"), lax.axis_size("ctx")
    count = feats.shape[1]
    blocks = count // BLK
    kept = blocks + n_ctx + 2
    operands = (
        feats.reshape(blocks, BLK, D), face_rows, neighbours.transpose(2, 0, 1).reshape(OFFSETS, blocks, 1, BLK), block_len, dilated.transpose(0, 2, 1), pick,
        cpe_weight.reshape(-1, D), cpe_bias[None], ln_gain[None], ln_bias[None], w_qkv, w_out,
    )
    operands = [pltpu.with_memory_space_constraint(operand, pltpu.HBM) for operand in operands]
    shape = lambda i: operands[i].shape
    return pl.pallas_call(
        functools.partial(body, n_space, n_ctx),
        in_specs=[pl.BlockSpec(memory_space=pltpu.HBM)] * len(operands),
        out_specs=pl.BlockSpec(memory_space=pltpu.VMEM),
        out_shape=jax.ShapeDtypeStruct((blocks, BLK, D), BF16),
        scratch_shapes=[
            pltpu.VMEM(((count + 2 * EDGE + 3 * FACE) // BLK, BLK, D), BF16),
            pltpu.VMEM(shape(1), jnp.int32),
            pltpu.VMEM(shape(2), jnp.int32),
            pltpu.VMEM(shape(6), BF16),
            pltpu.VMEM(shape(7), F32),
            pltpu.VMEM(shape(8), F32),
            pltpu.VMEM(shape(9), F32),
            pltpu.VMEM(shape(10), BF16),
            pltpu.VMEM(shape(11), BF16),
            pltpu.SMEM(shape(3), jnp.int32),
            pltpu.SMEM(shape(4), jnp.int32),
            pltpu.SMEM(shape(5), jnp.int32),
            pltpu.SMEM((blocks,), jnp.int32),
            pltpu.SMEM((blocks,), jnp.int32),
            pltpu.VMEM((EARLY, OFFSETS * BLK, D), BF16),
            pltpu.VMEM((blocks, BLK, D), F32),
            pltpu.VMEM((blocks, BLK, D), BF16),
            pltpu.VMEM((blocks, BLK, D), BF16),
            pltpu.VMEM((kept, BLK, D), BF16),
            pltpu.VMEM((kept, BLK, D), BF16),
            pltpu.VMEM((kept, BLK, HALF), BF16),
            pltpu.VMEM((n_ctx, BLK, D), BF16),
            pltpu.VMEM((2, BLK, D), BF16),
            pltpu.VMEM((n_ctx + 2, BLK, D), BF16),
            pltpu.VMEM((blocks - 2, BLK, D), F32),
            pltpu.VMEM((blocks - 2, BLK, D), F32),
            pltpu.VMEM((blocks - 2, BLK, D), F32),
            pltpu.SemaphoreType.DMA((len(operands),)),
            pltpu.SemaphoreType.DMA((4,)),
            pltpu.SemaphoreType.DMA((4,)),
            pltpu.SemaphoreType.DMA((n_ctx + 2,)),
            pltpu.SemaphoreType.DMA((n_ctx + 2,)),
        ],
        compiler_params=pltpu.CompilerParams(
            collective_id=0, has_side_effects=True, vmem_limit_bytes=48 * 2**20
        ),
    )(*operands).reshape(1, count, D)


def solution(mesh):
    placed = (
        P("space", "ctx", None),
        P("space", "ctx"),
        P("space", "ctx", None),
        P("space", None),
        P("space", "ctx", None),
        P("space", None, None),
        P(),
        P(),
        P(),
        P(),
        P(),
        P(),
    )
    return jax.shard_map(
        on_device, mesh=mesh, in_specs=placed, out_specs=P("space", "ctx", None), check_vma=False
    )
```

time: 59.1 us -> 39.5 us (0.67)
  the two profiles are of different devices: /device:TPU:16 before, /device:TPU:0 now
where the time goes in v1:
time: 39.5 us; the launch traced here: 38.9 us
  Pallas kernels  38.1 us (96%)
  local copies, waits for them, and re-layouts  0.8 us (2%)
    pallas_call x1, Pallas kernels, on_device(): pl.pallas_call(functools.partial(body, n_space, n_ctx), in_specs=[pl.Bloc...  38.1 us
    unnamed x1, local copies, waits for them, and re-layouts  0.8 us

profile of v1, /device:TPU:0, one launch (start us, length us, event | category | flops | bytes accessed | tf_op | source)
XLA Modules:
  0.0 38.9 jit_solution(9672221102834506153)
XLA Ops:
  0.0 38.1 %shard_map.118 = bf16[8,128,256]{2,1,0:T(8,128)(2,1)S(1)} custom-call(bf16[8,128,256]{2,1,0:T(8,128)(2,1)} %bitcast.12, s32[1,256]{1,0:T(1,128)} %face_rows.1, s32[6,8,1,128]{3,2,1,0:T(1,128)} %bitcast.13, s32[1,64]{1,0:T(1,128)} %block_len.1, s32[1,4,8]{2,1,0:T(4,128)} %bitcast.14, s32[1,8,8]{2,1,0:T(8,128)} %pick.1, bf16[1792,256]{1,0:T(8,128)(2,1)} %bitcast.11, ...), custom_call_target="tpu_custom_call" | custom-call | tf_op jit(solution)/shard_map/pallas_call | solution.py:396
  38.1 0.8 %copy.14 = bf16[1,1024,256]{2,1,0:T(8,128)(2,1)} copy(bf16[1,1024,256]{2,1,0:T(8,128)(2,1)S(1)} %bitcast.10) | data formatting | bytes 1048576

commit v2 on v1

--- a/solution.py
+++ b/solution.py
@@ -23,6 +23,7 @@
 LOCAL_PARTS = tuple(range(1, 9)) + (12, 13)
 SENT_PARTS = (0, 9, 10, 11, 14, 15)
 EARLY = 4
+FIRST = 4
 
 
 def zero_like(value):
@@ -35,8 +36,8 @@
     out_ref,
     table, rows_v, ids_v, weight_v, bias_v, gain_v, shift_v, qkv_v, outw_v,
     lens_s, slots_s, pick_s, pos_s, perm_s,
-    early, hidden_s, query_s, normed_s, key_s, value_s, ones_s, outgoing, ends, far,
-    near_peak, near_sum, near_den,
+    hidden_s, query_s, normed_s, key_s, value_s, ones_s, outgoing, ends, far,
+    near_peak, near_sum, near_den, picked_s, scores_a, scores_b,
     load_sem, table_send, table_recv, send_sem, recv_sem,
 ):
     space, ctx = lax.axis_index("space"), lax.axis_index("ctx")
@@ -44,6 +45,7 @@
     count = blocks * BLK
     local = count + FACE
 
+    scores_s = (scores_a, scores_b)
     barrier = pltpu.get_barrier_semaphore()
 
     def ctx_peer(j):
@@ -83,7 +85,7 @@
             (w_out, outw_v),
         ))
     ]
-    for load in loads:
+    for load in loads[:FIRST]:
         load.start()
 
     lane = lax.broadcasted_iota(jnp.int32, (BLK, HALF), 1)
@@ -105,6 +107,8 @@
         choose(hot, high, range(blocks)), table[:blocks].reshape(count, D), preferred_element_type=F32
     ).astype(BF16).reshape(FACE // BLK, BLK, D)
 
+    for load in loads[FIRST:]:
+        load.start()
     pl.semaphore_wait(
         barrier, n_ctx - 1 + sides[2][0].astype(jnp.int32) + sides[3][0].astype(jnp.int32)
     )
@@ -160,7 +164,7 @@
 
     def pick_early(j, carry):
         hot, high = step_ids(j)
-        early[j] = jnp.dot(
+        picked_s[j] = jnp.dot(
             choose(hot, high, LOCAL_PARTS), table_rows(0, local), preferred_element_type=F32
         ).astype(BF16)
         return carry
@@ -191,41 +195,55 @@
         outgoing[j] = block_at(normed_s, pos_s[pick_s[0, ctx, ctx_peer(j)]])
         send(j).start()
 
-    def finish(j, picked):
-        block = perm_s[j]
-        own = block_at(table, block)
-        taps = jnp.concatenate([own] + [picked[o * BLK : (o + 1) * BLK] for o in range(OFFSETS)], 1)
+    def finish(first, last):
+        steps = range(first, last)
+        order = [perm_s[j] for j in steps]
+        own = jnp.concatenate([table[block] for block in order], 0)
+        taps = jnp.concatenate(
+            [own]
+            + [jnp.concatenate([picked_s[j, o * BLK : (o + 1) * BLK] for j in steps], 0) for o in range(OFFSETS)],
+            1,
+        )
         conv = jnp.dot(taps, weight_v[...], preferred_element_type=F32)
         hidden = own.astype(F32) + conv + bias_v[...]
-        hidden_s[j] = hidden
         center = hidden - jnp.mean(hidden, axis=-1, keepdims=True)
         variance = jnp.mean(center * center, axis=-1, keepdims=True)
         normed = (center * lax.rsqrt(variance + 1e-05) * gain_v[...] + shift_v[...]).astype(BF16)
-        normed_s[j] = normed
+        for b, j in enumerate(steps):
+            normed_s[j] = normed[b * BLK : (b + 1) * BLK]
+        for j in steps:
+            if j < n_ctx - 1:
+                start_send(j)
         projected = jnp.dot(normed, qkv_v[...], preferred_element_type=F32)
-        query_s[j] = projected[:, :D].astype(BF16)
-        keys = projected[:, D : 2 * D]
-        keep(j, keys, projected[:, 2 * D :], lens_s[0, ctx * blocks + block], keys[:1])
-
-        @pl.when(j < n_ctx - 1)
-        def _():
-            start_send(j)
-
-    def finish_early(j, carry):
+        for b, j in enumerate(steps):
+            part = slice(b * BLK, (b + 1) * BLK)
+            hidden_s[j] = hidden[part]
+            query_s[j] = projected[part, :D].astype(BF16)
+            keys = projected[part, D : 2 * D]
+            keep(j, keys, projected[part, 2 * D :], lens_s[0, ctx * blocks + order[b]], keys[:1])
+
+    def pick_sent(j, carry):
         hot, high = step_ids(j)
-        sent = jnp.dot(choose(hot, high, SENT_PARTS), table_rows(local, table.shape[0] * BLK), preferred_element_type=F32)
-        mine = early[j]
-        finish(j, (sent + mine.astype(F32)).astype(BF16))
-        return carry
-
-    def finish_late(j, carry):
+        sent = jnp.dot(
+            choose(hot, high, SENT_PARTS), table_rows(local, table.shape[0] * BLK), preferred_element_type=F32
+        )
+        picked_s[j] = (sent + picked_s[j].astype(F32)).astype(BF16)
+        return carry
+
+    def pick_late(j, carry):
         hot, high = step_ids(j)
-        picked = jnp.dot(choose(hot, high, LOCAL_PARTS + SENT_PARTS), table_rows(0, table.shape[0] * BLK), preferred_element_type=F32)
-        finish(j, picked.astype(BF16))
-        return carry
-
-    lax.fori_loop(0, EARLY, finish_early, 0)
-    lax.fori_loop(EARLY, blocks, finish_late, 0)
+        picked_s[j] = jnp.dot(
+            choose(hot, high, LOCAL_PARTS + SENT_PARTS), table_rows(0, table.shape[0] * BLK),
+            preferred_element_type=F32,
+        ).astype(BF16)
+        return carry
+
+    lax.fori_loop(0, 1, pick_sent, 0)
+    finish(0, 1)
+    lax.fori_loop(1, EARLY, pick_sent, 0)
+    finish(1, EARLY)
+    lax.fori_loop(EARLY, blocks, pick_late, 0)
+    finish(EARLY, blocks)
 
     ends[0] = block_at(normed_s, pos_s[0])
     ends[1] = block_at(normed_s, pos_s[blocks - 1])
@@ -264,72 +282,71 @@
             result = part if result is None else jnp.where(head_of == head, part, result)
         return result
 
-    def attend(query, sources):
-        def stack(ref, group):
-            cols = slice(group * HALF, (group + 1) * HALF)
-            return jnp.concatenate([ref[index, :, cols] for index in sources], 0)
-
-        def score(group):
-            part = query[:, group * HALF : (group + 1) * HALF]
-            stacked = jnp.concatenate(
-                [jnp.where(head_of == head, part, zero_like(part)) for head in range(heads)], 0
-            )
-            return lax.dot_general(
-                stacked, stack(key_s, group), (((1,), (1,)), ((), ())), preferred_element_type=F32
-            )
-
-        ones = jnp.concatenate([block_at(ones_s, index) for index in sources], 0)
-        results = []
-        scores = [score(group) for group in range(groups)]
-        for group in range(groups):
-            peak = jnp.max(scores[group], axis=-1, keepdims=True)
-            weights = jnp.exp2((scores[group] - peak) * scale).astype(BF16)
-            mixed = jnp.dot(
-                weights, jnp.concatenate([stack(value_s, group), ones], 1), preferred_element_type=F32
-            )
-            results.append((peak, mixed[:, :HALF], mixed[:, HALF:]))
-        return results
+    def stack(ref, sources, group):
+        cols = slice(group * HALF, (group + 1) * HALF)
+        return jnp.concatenate([ref[index, :, cols] for index in sources], 0)
+
+    def score(at, sources, group):
+        part = query_s[at, :, group * HALF : (group + 1) * HALF]
+        stacked = jnp.concatenate(
+            [jnp.where(head_of == head, part, zero_like(part)) for head in range(heads)], 0
+        )
+        scores_s[group][:, : len(sources) * BLK] = lax.dot_general(
+            stacked, stack(key_s, sources, group), (((1,), (1,)), ((), ())), preferred_element_type=F32
+        )
+
+    def weigh(sources, group):
+        scores = scores_s[group][:, : len(sources) * BLK]
+        peak = jnp.max(scores, axis=-1, keepdims=True)
+        weights = jnp.exp2((scores - peak) * scale).astype(BF16)
+        ones = jnp.concatenate([ones_s[index] for index in sources], 0)
+        mixed = jnp.dot(
+            weights, jnp.concatenate([stack(value_s, sources, group), ones], 1), preferred_element_type=F32
+        )
+        return peak, mixed[:, :HALF], mixed[:, HALF:]
+
+    def attend(at, sources, then):
+        score(at, sources, 1)
+        first = weigh(sources, 0)
+        if then is not None:
+            score(*then, 0)
+        return [first, weigh(sources, 1)]
 
     def near_blocks(b):
         return [pos_s[b - 1], pos_s[b], pos_s[b + 1]]
 
     def near(i, carry):
         b = i + 1
+        after = jnp.minimum(b + 1, blocks - 2)
         at = pos_s[b]
-        for group, (peak, total, den) in enumerate(attend(block_at(query_s, at), near_blocks(b))):
+        for group, (peak, total, den) in enumerate(attend(at, near_blocks(b), (pos_s[after], near_blocks(after)))):
             cols = slice(group * HALF, (group + 1) * HALF)
             near_peak[i, :, cols] = spread(peak)
             near_sum[i, :, cols] = spread(total)
             near_den[i, :, cols] = spread(den)
         return carry
 
+    score(pos_s[1], near_blocks(1), 0)
     lax.fori_loop(0, blocks - 2, near, 0)
 
     for j in range(n_ctx - 1):
         send(j).wait()
-    for side, edge in zip(sides[:2], edges):
-        pl.when(side[0])(edge.wait_send)
-        pl.when(side[1])(edge.wait_recv)
 
     left, right = blocks + n_ctx, blocks + n_ctx + 1
 
-    def project(s, valid, spare):
-        both = jnp.dot(far[s], qkv_v[:, D:], preferred_element_type=F32)
+    def project(first, last):
+        return jnp.dot(
+            far[first:last].reshape((last - first) * BLK, D), qkv_v[:, D:], preferred_element_type=F32
+        )
+
+    def keep_far(s, both, valid, spare):
         keys = both[:, :D]
         keep(blocks + s, keys, both[:, D:], valid, keys[:1] if spare is None else spare)
 
-    def project_far(s, carry):
-        project(s, lens_s[0, s * blocks + pick_s[0, s, ctx]], None)
-        return carry
-
-    lax.fori_loop(0, n_ctx, project_far, 0)
-    for s, there, at, inner in (
-        (n_ctx, ctx > 0, ctx * blocks - 1, 0),
-        (n_ctx + 1, ctx < n_ctx - 1, (ctx + 1) * blocks, blocks - 1),
-    ):
-        valid = jnp.where(there, lens_s[0, jnp.where(there, at, 0)], 0)
-        project(s, valid, block_at(key_s, pos_s[inner])[:1].astype(F32))
-
+    arrived = project(0, n_ctx)
+
+    for s in range(n_ctx):
+        keep_far(s, arrived[s * BLK : (s + 1) * BLK], lens_s[0, s * blocks + pick_s[0, s, ctx]], None)
     def far_blocks(b):
         return [blocks + slots_s[0, k, b] for k in range(slots_s.shape[1])]
 
@@ -341,9 +358,10 @@
 
     def far_inner(i, carry):
         b = i + 1
+        after = jnp.minimum(b + 1, blocks - 2)
         at = pos_s[b]
         attended = []
-        for group, (peak, total, den) in enumerate(attend(block_at(query_s, at), far_blocks(b))):
+        for group, (peak, total, den) in enumerate(attend(at, far_blocks(b), (pos_s[after], far_blocks(after)))):
             cols = slice(group * HALF, (group + 1) * HALF)
             peak, other = spread(peak), near_peak[i, :, cols]
             top = jnp.maximum(peak, other)
@@ -355,15 +373,28 @@
         write(b, at, attended)
         return carry
 
+    score(pos_s[1], far_blocks(1), 0)
     lax.fori_loop(0, blocks - 2, far_inner, 0)
+
+    for side, edge in zip(sides[:2], edges):
+        pl.when(side[0])(edge.wait_send)
+        pl.when(side[1])(edge.wait_recv)
+    arrived = project(n_ctx, n_ctx + 2)
+    for s, there, at, inner in (
+        (n_ctx, ctx > 0, ctx * blocks - 1, 0),
+        (n_ctx + 1, ctx < n_ctx - 1, (ctx + 1) * blocks, blocks - 1),
+    ):
+        valid = jnp.where(there, lens_s[0, jnp.where(there, at, 0)], 0)
+        keep_far(s, arrived[(s - n_ctx) * BLK : (s - n_ctx + 1) * BLK], valid, block_at(key_s, pos_s[inner])[:1].astype(F32))
 
     def whole(i, carry):
         b = i * (blocks - 1)
-        at = pos_s[b]
         before = jnp.where(i == 0, left, pos_s[jnp.maximum(b - 1, 0)])
         after = jnp.where(i == 0, pos_s[jnp.minimum(b + 1, blocks - 1)], right)
-        results = attend(block_at(query_s, at), [before, at, after] + far_blocks(b))
-        write(b, at, [spread(total) / spread(den) for _, total, den in results])
+        sources = [before, pos_s[b], after] + far_blocks(b)
+        score(pos_s[b], sources, 0)
+        results = attend(pos_s[b], sources, None)
+        write(b, pos_s[b], [spread(total) / spread(den) for _, total, den in results])
         return carry
 
     lax.fori_loop(0, 2, whole, 0)
@@ -413,7 +444,6 @@
             pltpu.SMEM(shape(5), jnp.int32),
             pltpu.SMEM((blocks,), jnp.int32),
             pltpu.SMEM((blocks,), jnp.int32),
-            pltpu.VMEM((EARLY, OFFSETS * BLK, D), BF16),
             pltpu.VMEM((blocks, BLK, D), F32),
             pltpu.VMEM((blocks, BLK, D), BF16),
             pltpu.VMEM((blocks, BLK, D), BF16),
@@ -426,6 +456,9 @@
             pltpu.VMEM((blocks - 2, BLK, D), F32),
             pltpu.VMEM((blocks - 2, BLK, D), F32),
             pltpu.VMEM((blocks - 2, BLK, D), F32),
+            pltpu.VMEM((blocks, OFFSETS * BLK, D), BF16),
+            pltpu.VMEM((HALF * HEADS // D * BLK, 7 * BLK), F32),
+            pltpu.VMEM((HALF * HEADS // D * BLK, 7 * BLK), F32),
             pltpu.SemaphoreType.DMA((len(operands),)),
             pltpu.SemaphoreType.DMA((4,)),
             pltpu.SemaphoreType.DMA((4,)),

time: 39.5 us -> 37.4 us (0.947)
  Pallas kernels: 38.1 us -> 36.4 us
    pallas_call x1, Pallas kernels: 38.1 us -> 36.4 us  [on_device(): pl.pallas_call(functools.partial(body, n_space, n_ctx), in_specs=[pl.Bloc...]
where the time goes in v2:
time: 37.4 us; the launch traced here: 37.2 us
  Pallas kernels  36.4 us (97%)
  local copies, waits for them, and re-layouts  0.8 us (2%)
    pallas_call x1, Pallas kernels, on_device(): pl.pallas_call(functools.partial(body, n_space, n_ctx), in_specs=[pl.Bloc...  36.4 us
    unnamed x1, local copies, waits for them, and re-layouts  0.8 us

profile of v2, /device:TPU:0, one launch (start us, length us, event | category | flops | bytes accessed | tf_op | source)
XLA Modules:
  0.0 37.2 jit_solution(5845586450290568822)
XLA Ops:
  0.0 36.4 %shard_map.118 = bf16[8,128,256]{2,1,0:T(8,128)(2,1)S(1)} custom-call(bf16[8,128,256]{2,1,0:T(8,128)(2,1)} %bitcast.12, s32[1,256]{1,0:T(1,128)} %face_rows.1, s32[6,8,1,128]{3,2,1,0:T(1,128)} %bitcast.13, s32[1,64]{1,0:T(1,128)} %block_len.1, s32[1,4,8]{2,1,0:T(4,128)} %bitcast.14, s32[1,8,8]{2,1,0:T(8,128)} %pick.1, bf16[1792,256]{1,0:T(8,128)(2,1)} %bitcast.11, ...), custom_call_target="tpu_custom_call" | custom-call | tf_op jit(solution)/shard_map/pallas_call | solution.py:427
  36.4 0.8 %copy.14 = bf16[1,1024,256]{2,1,0:T(8,128)(2,1)} copy(bf16[1,1024,256]{2,1,0:T(8,128)(2,1)S(1)} %bitcast.10) | data formatting | bytes 1048576

commit v3 on v2

--- a/solution.py
+++ b/solution.py
@@ -22,8 +22,8 @@
 
 LOCAL_PARTS = tuple(range(1, 9)) + (12, 13)
 SENT_PARTS = (0, 9, 10, 11, 14, 15)
-EARLY = 4
-FIRST = 4
+EARLY = 6
+GROUPS = (1, 4, 8)
 
 
 def zero_like(value):
@@ -37,7 +37,7 @@
     table, rows_v, ids_v, weight_v, bias_v, gain_v, shift_v, qkv_v, outw_v,
     lens_s, slots_s, pick_s, pos_s, perm_s,
     hidden_s, query_s, normed_s, key_s, value_s, ones_s, outgoing, ends, far,
-    near_peak, near_sum, near_den, picked_s, scores_a, scores_b,
+    near_peak, near_sum, near_den, picked_s, hot_s, high_s, scores_a, scores_b,
     load_sem, table_send, table_recv, send_sem, recv_sem,
 ):
     space, ctx = lax.axis_index("space"), lax.axis_index("ctx")
@@ -49,11 +49,8 @@
     barrier = pltpu.get_barrier_semaphore()
 
     def ctx_peer(j):
-        half = n_ctx // 2
-        mine = ctx // half
-        other = (1 - mine) * half + lax.rem(ctx + j, half)
-        same = mine * half + lax.rem(ctx + j + 1, half)
-        return jnp.where(j < half, other, same)
+        turn = (j + 1) // 2
+        return lax.rem(ctx + n_ctx // 2 + (n_ctx - turn if j % 2 else turn), n_ctx)
 
     for j in range(n_ctx - 1):
         pl.semaphore_signal(barrier, inc=1, device_id=(space, ctx_peer(j)), device_id_type=MESH)
@@ -85,7 +82,7 @@
             (w_out, outw_v),
         ))
     ]
-    for load in loads[:FIRST]:
+    for load in loads:
         load.start()
 
     lane = lax.broadcasted_iota(jnp.int32, (BLK, HALF), 1)
@@ -107,8 +104,6 @@
         choose(hot, high, range(blocks)), table[:blocks].reshape(count, D), preferred_element_type=F32
     ).astype(BF16).reshape(FACE // BLK, BLK, D)
 
-    for load in loads[FIRST:]:
-        load.start()
     pl.semaphore_wait(
         barrier, n_ctx - 1 + sides[2][0].astype(jnp.int32) + sides[3][0].astype(jnp.int32)
     )
@@ -163,13 +158,13 @@
         return split_ids([ids_v[o, at] for o in range(OFFSETS)])
 
     def pick_early(j, carry):
-        hot, high = step_ids(j)
+        hot, high = hot_s[j], high_s[j] = step_ids(j)
         picked_s[j] = jnp.dot(
             choose(hot, high, LOCAL_PARTS), table_rows(0, local), preferred_element_type=F32
         ).astype(BF16)
         return carry
 
-    lax.fori_loop(0, EARLY, pick_early, 0)
+    lax.fori_loop(0, EARLY, pick_early, 0, unroll=2)
 
     for i in range(4):
         pl.when(sides[i][0])(copies[i].wait_send)
@@ -223,7 +218,7 @@
             keep(j, keys, projected[part, 2 * D :], lens_s[0, ctx * blocks + order[b]], keys[:1])
 
     def pick_sent(j, carry):
-        hot, high = step_ids(j)
+        hot, high = hot_s[j], high_s[j]
         sent = jnp.dot(
             choose(hot, high, SENT_PARTS), table_rows(local, table.shape[0] * BLK), preferred_element_type=F32
         )
@@ -238,12 +233,14 @@
         ).astype(BF16)
         return carry
 
-    lax.fori_loop(0, 1, pick_sent, 0)
-    finish(0, 1)
-    lax.fori_loop(1, EARLY, pick_sent, 0)
-    finish(1, EARLY)
-    lax.fori_loop(EARLY, blocks, pick_late, 0)
-    finish(EARLY, blocks)
+    first = 0
+    for last in GROUPS:
+        if first < EARLY:
+            lax.fori_loop(first, min(last, EARLY), pick_sent, 0, unroll=True)
+        if last > EARLY:
+            lax.fori_loop(max(first, EARLY), last, pick_late, 0, unroll=2)
+        finish(first, last)
+        first = last
 
     ends[0] = block_at(normed_s, pos_s[0])
     ends[1] = block_at(normed_s, pos_s[blocks - 1])
@@ -260,8 +257,8 @@
     ]
     for side, edge in zip(sides[:2], edges):
         pl.when(side[0])(edge.start)
-    if n_ctx - 1 > blocks:
-        lax.fori_loop(blocks, n_ctx - 1, lambda j, carry: (start_send(j), carry)[1], 0)
+    for j in range(blocks, n_ctx - 1):
+        start_send(j)
     far[ctx] = block_at(normed_s, pos_s[pick_s[0, ctx, ctx]])
     for i, side in enumerate(sides[:2]):
         @pl.when(jnp.logical_not(side[1]))
@@ -327,7 +324,7 @@
         return carry
 
     score(pos_s[1], near_blocks(1), 0)
-    lax.fori_loop(0, blocks - 2, near, 0)
+    lax.fori_loop(0, blocks - 2, near, 0, unroll=2)
 
     for j in range(n_ctx - 1):
         send(j).wait()
@@ -374,7 +371,7 @@
         return carry
 
     score(pos_s[1], far_blocks(1), 0)
-    lax.fori_loop(0, blocks - 2, far_inner, 0)
+    lax.fori_loop(0, blocks - 2, far_inner, 0, unroll=2)
 
     for side, edge in zip(sides[:2], edges):
         pl.when(side[0])(edge.wait_send)
@@ -457,6 +454,8 @@
             pltpu.VMEM((blocks - 2, BLK, D), F32),
             pltpu.VMEM((blocks - 2, BLK, D), F32),
             pltpu.VMEM((blocks, OFFSETS * BLK, D), BF16),
+            pltpu.VMEM((EARLY, OFFSETS * BLK, HALF), BF16),
+            pltpu.VMEM((EARLY, OFFSETS * BLK, HALF), BF16),
             pltpu.VMEM((HALF * HEADS // D * BLK, 7 * BLK), F32),
             pltpu.VMEM((HALF * HEADS // D * BLK, 7 * BLK), F32),
             pltpu.SemaphoreType.DMA((len(operands),)),

time: 37.4 us -> 34.1 us (0.912)
  Pallas kernels: 36.4 us -> 33.1 us
    pallas_call x1, Pallas kernels: 36.4 us -> 33.1 us  [on_device(): pl.pallas_call(functools.partial(body, n_space, n_ctx), in_specs=[pl.Bloc...]
where the time goes in v3:
time: 34.1 us; the launch traced here: 33.9 us
  Pallas kernels  33.1 us (97%)
  local copies, waits for them, and re-layouts  0.8 us (2%)
    pallas_call x1, Pallas kernels, on_device(): pl.pallas_call(functools.partial(body, n_space, n_ctx), in_specs=[pl.Bloc...  33.1 us
    unnamed x1, local copies, waits for them, and re-layouts  0.8 us

profile of v3, /device:TPU:0, one launch (start us, length us, event | category | flops | bytes accessed | tf_op | source)
XLA Modules:
  0.0 33.9 jit_solution(8509073776890587726)
XLA Ops:
  0.0 33.1 %shard_map.118 = bf16[8,128,256]{2,1,0:T(8,128)(2,1)S(1)} custom-call(bf16[8,128,256]{2,1,0:T(8,128)(2,1)} %bitcast.12, s32[1,256]{1,0:T(1,128)} %face_rows.1, s32[6,8,1,128]{3,2,1,0:T(1,128)} %bitcast.13, s32[1,64]{1,0:T(1,128)} %block_len.1, s32[1,4,8]{2,1,0:T(4,128)} %bitcast.14, s32[1,8,8]{2,1,0:T(8,128)} %pick.1, bf16[1792,256]{1,0:T(8,128)(2,1)} %bitcast.11, ...), custom_call_target="tpu_custom_call" | custom-call | tf_op jit(solution)/shard_map/pallas_call | solution.py:424
  33.1 0.8 %copy.14 = bf16[1,1024,256]{2,1,0:T(8,128)(2,1)} copy(bf16[1,1024,256]{2,1,0:T(8,128)(2,1)S(1)} %bitcast.10) | data formatting | bytes 1048576

commit v4 on v3

--- a/solution.py
+++ b/solution.py
@@ -97,40 +97,6 @@
     def choose(hot, high, parts):
         return jnp.concatenate([jnp.where(high == BF16(part), hot, zero_like(hot)) for part in parts], 1)
 
-    loads[0].wait()
-    loads[1].wait()
-    hot, high = split_ids([rows_v[:, i * BLK : (i + 1) * BLK] for i in range(FACE // BLK)])
-    table[blocks : local // BLK] = jnp.dot(
-        choose(hot, high, range(blocks)), table[:blocks].reshape(count, D), preferred_element_type=F32
-    ).astype(BF16).reshape(FACE // BLK, BLK, D)
-
-    pl.semaphore_wait(
-        barrier, n_ctx - 1 + sides[2][0].astype(jnp.int32) + sides[3][0].astype(jnp.int32)
-    )
-    pieces = (
-        (count - EDGE, local, EDGE),
-        (0, local + EDGE, EDGE),
-        (count, local + 2 * EDGE, FACE),
-        (count, local + 2 * EDGE + FACE, FACE),
-    )
-    copies = [
-        pltpu.make_async_remote_copy(
-            src_ref=table.at[pl.ds(source // BLK, size // BLK)],
-            dst_ref=table.at[pl.ds(target // BLK, size // BLK)],
-            send_sem=table_send.at[i],
-            recv_sem=table_recv.at[i],
-            device_id=sides[i][2],
-            device_id_type=MESH,
-        )
-        for i, (source, target, size) in enumerate(pieces)
-    ]
-    for i in (2, 3, 0, 1):
-        pl.when(sides[i][0])(copies[i].start)
-    for i, (_, target, size) in enumerate(pieces):
-        @pl.when(jnp.logical_not(sides[i][1]))
-        def _():
-            table[target // BLK : (target + size) // BLK] = jnp.zeros((size // BLK, BLK, D), BF16)
-
     loads[2].wait()
     wanted = [pick_s[0, ctx, ctx_peer(j)] for j in range(n_ctx)]
     need = [jnp.int32(n_ctx + b) for b in range(blocks)]
@@ -143,6 +109,40 @@
         pos_s[b] = position[b]
     for j in range(blocks):
         perm_s[j] = sum(jnp.where(position[b] == j, b, 0) for b in range(blocks))
+
+    loads[0].wait()
+    loads[1].wait()
+    hot, high = split_ids([rows_v[:, i * BLK : (i + 1) * BLK] for i in range(FACE // BLK)])
+    table[blocks : local // BLK] = jnp.dot(
+        choose(hot, high, range(blocks)), table[:blocks].reshape(count, D), preferred_element_type=F32
+    ).astype(BF16).reshape(FACE // BLK, BLK, D)
+
+    pl.semaphore_wait(
+        barrier, n_ctx - 1 + sides[2][0].astype(jnp.int32) + sides[3][0].astype(jnp.int32)
+    )
+    pieces = (
+        (count - EDGE, local, EDGE),
+        (0, local + EDGE, EDGE),
+        (count, local + 2 * EDGE, FACE),
+        (count, local + 2 * EDGE + FACE, FACE),
+    )
+    copies = [
+        pltpu.make_async_remote_copy(
+            src_ref=table.at[pl.ds(source // BLK, size // BLK)],
+            dst_ref=table.at[pl.ds(target // BLK, size // BLK)],
+            send_sem=table_send.at[i],
+            recv_sem=table_recv.at[i],
+            device_id=sides[i][2],
+            device_id_type=MESH,
+        )
+        for i, (source, target, size) in enumerate(pieces)
+    ]
+    for i in (2, 3, 0, 1):
+        pl.when(sides[i][0])(copies[i].start)
+    for i, (_, target, size) in enumerate(pieces):
+        @pl.when(jnp.logical_not(sides[i][1]))
+        def _():
+            table[target // BLK : (target + size) // BLK] = jnp.zeros((size // BLK, BLK, D), BF16)
 
     for load in loads[3:]:
         load.wait()
@@ -312,19 +312,25 @@
     def near_blocks(b):
         return [pos_s[b - 1], pos_s[b], pos_s[b + 1]]
 
-    def near(i, carry):
-        b = i + 1
-        after = jnp.minimum(b + 1, blocks - 2)
-        at = pos_s[b]
-        for group, (peak, total, den) in enumerate(attend(at, near_blocks(b), (pos_s[after], near_blocks(after)))):
+    def keep_near(i, results):
+        for group, (peak, total, den) in enumerate(results):
             cols = slice(group * HALF, (group + 1) * HALF)
             near_peak[i, :, cols] = spread(peak)
             near_sum[i, :, cols] = spread(total)
             near_den[i, :, cols] = spread(den)
+
+    def near(i, carry):
+        b = i + 1
+        after = jnp.minimum(b + 1, blocks - 2)
+        keep_near(i, attend(pos_s[b], near_blocks(b), (pos_s[after], near_blocks(after))))
         return carry
 
     score(pos_s[1], near_blocks(1), 0)
-    lax.fori_loop(0, blocks - 2, near, 0, unroll=2)
+    lax.fori_loop(0, blocks - 2, near, 0, unroll=3)
+    for i, (b, own) in enumerate(((0, (0, 1)), (blocks - 1, (blocks - 2, blocks - 1)))):
+        sources = [pos_s[c] for c in own]
+        score(pos_s[b], sources, 0)
+        keep_near(blocks - 2 + i, attend(pos_s[b], sources, None))
 
     for j in range(n_ctx - 1):
         send(j).wait()
@@ -353,12 +359,9 @@
             + jnp.dot(jnp.concatenate(attended, 1).astype(BF16), outw_v[...], preferred_element_type=F32)
         ).astype(BF16)
 
-    def far_inner(i, carry):
-        b = i + 1
-        after = jnp.minimum(b + 1, blocks - 2)
-        at = pos_s[b]
+    def merge(b, i, results):
         attended = []
-        for group, (peak, total, den) in enumerate(attend(at, far_blocks(b), (pos_s[after], far_blocks(after)))):
+        for group, (peak, total, den) in enumerate(results):
             cols = slice(group * HALF, (group + 1) * HALF)
             peak, other = spread(peak), near_peak[i, :, cols]
             top = jnp.maximum(peak, other)
@@ -367,11 +370,16 @@
                 (spread(total) * mine + near_sum[i, :, cols] * theirs)
                 / (spread(den) * mine + near_den[i, :, cols] * theirs)
             )
-        write(b, at, attended)
+        write(b, pos_s[b], attended)
+
+    def far_inner(i, carry):
+        b = i + 1
+        after = jnp.minimum(b + 1, blocks - 2)
+        merge(b, i, attend(pos_s[b], far_blocks(b), (pos_s[after], far_blocks(after))))
         return carry
 
     score(pos_s[1], far_blocks(1), 0)
-    lax.fori_loop(0, blocks - 2, far_inner, 0, unroll=2)
+    lax.fori_loop(0, blocks - 2, far_inner, 0, unroll=3)
 
     for side, edge in zip(sides[:2], edges):
         pl.when(side[0])(edge.wait_send)
@@ -384,17 +392,10 @@
         valid = jnp.where(there, lens_s[0, jnp.where(there, at, 0)], 0)
         keep_far(s, arrived[(s - n_ctx) * BLK : (s - n_ctx + 1) * BLK], valid, block_at(key_s, pos_s[inner])[:1].astype(F32))
 
-    def whole(i, carry):
-        b = i * (blocks - 1)
-        before = jnp.where(i == 0, left, pos_s[jnp.maximum(b - 1, 0)])
-        after = jnp.where(i == 0, pos_s[jnp.minimum(b + 1, blocks - 1)], right)
-        sources = [before, pos_s[b], after] + far_blocks(b)
+    for i, (b, end) in enumerate(((0, left), (blocks - 1, right))):
+        sources = [end] + far_blocks(b)
         score(pos_s[b], sources, 0)
-        results = attend(pos_s[b], sources, None)
-        write(b, pos_s[b], [spread(total) / spread(den) for _, total, den in results])
-        return carry
-
-    lax.fori_loop(0, 2, whole, 0)
+        merge(b, blocks - 2 + i, attend(pos_s[b], sources, None))
 
 
 def on_device(
@@ -450,9 +451,9 @@
             pltpu.VMEM((n_ctx, BLK, D), BF16),
             pltpu.VMEM((2, BLK, D), BF16),
             pltpu.VMEM((n_ctx + 2, BLK, D), BF16),
-            pltpu.VMEM((blocks - 2, BLK, D), F32),
-            pltpu.VMEM((blocks - 2, BLK, D), F32),
-            pltpu.VMEM((blocks - 2, BLK, D), F32),
+            pltpu.VMEM((blocks, BLK, D), F32),
+            pltpu.VMEM((blocks, BLK, D), F32),
+            pltpu.VMEM((blocks, BLK, D), F32),
             pltpu.VMEM((blocks, OFFSETS * BLK, D), BF16),
             pltpu.VMEM((EARLY, OFFSETS * BLK, HALF), BF16),
             pltpu.VMEM((EARLY, OFFSETS * BLK, HALF), BF16),

time: 34.1 us -> 33.2 us (0.974)
  Pallas kernels: 33.1 us -> 32.2 us
    pallas_call x1, Pallas kernels: 33.1 us -> 32.2 us  [on_device(): pl.pallas_call(functools.partial(body, n_space, n_ctx), in_specs=[pl.Bloc...]
where the time goes in v4:
time: 33.2 us; the launch traced here: 33 us
  Pallas kernels  32.2 us (97%)
  local copies, waits for them, and re-layouts  0.8 us (2%)
    pallas_call x1, Pallas kernels, on_device(): pl.pallas_call(functools.partial(body, n_space, n_ctx), in_specs=[pl.Bloc...  32.2 us
    unnamed x1, local copies, waits for them, and re-layouts  0.8 us

profile of v4, /device:TPU:0, one launch (start us, length us, event | category | flops | bytes accessed | tf_op | source)
XLA Modules:
  0.0 33.0 jit_solution(14852685759415413663)
XLA Ops:
  0.0 32.2 %shard_map.118 = bf16[8,128,256]{2,1,0:T(8,128)(2,1)S(1)} custom-call(bf16[8,128,256]{2,1,0:T(8,128)(2,1)} %bitcast.12, s32[1,256]{1,0:T(1,128)} %face_rows.1, s32[6,8,1,128]{3,2,1,0:T(1,128)} %bitcast.13, s32[1,64]{1,0:T(1,128)} %block_len.1, s32[1,4,8]{2,1,0:T(4,128)} %bitcast.14, s32[1,8,8]{2,1,0:T(8,128)} %pick.1, bf16[1792,256]{1,0:T(8,128)(2,1)} %bitcast.11, ...), custom_call_target="tpu_custom_call" | custom-call | tf_op jit(solution)/shard_map/pallas_call | solution.py:425
  32.2 0.8 %copy.14 = bf16[1,1024,256]{2,1,0:T(8,128)(2,1)} copy(bf16[1,1024,256]{2,1,0:T(8,128)(2,1)S(1)} %bitcast.10) | data formatting | bytes 1048576

commit v5 on v4

--- a/solution.py
+++ b/solution.py
@@ -379,7 +379,7 @@
         return carry
 
     score(pos_s[1], far_blocks(1), 0)
-    lax.fori_loop(0, blocks - 2, far_inner, 0, unroll=3)
+    lax.fori_loop(0, blocks - 2, far_inner, 0, unroll=True)
 
     for side, edge in zip(sides[:2], edges):
         pl.when(side[0])(edge.wait_send)

time: 33.2 us -> 32.8 us (0.988)
    pallas_call x1, Pallas kernels: 32.2 us -> 31.9 us  [on_device(): pl.pallas_call(functools.partial(body, n_space, n_ctx), in_specs=[pl.Bloc...]
where the time goes in v5:
time: 32.8 us; the launch traced here: 32.7 us
  Pallas kernels  31.9 us (97%)
  local copies, waits for them, and re-layouts  0.8 us (2%)
    pallas_call x1, Pallas kernels, on_device(): pl.pallas_call(functools.partial(body, n_space, n_ctx), in_specs=[pl.Bloc...  31.9 us
    unnamed x1, local copies, waits for them, and re-layouts  0.8 us

profile of v5, /device:TPU:0, one launch (start us, length us, event | category | flops | bytes accessed | tf_op | source)
XLA Modules:
  0.0 32.7 jit_solution(10921856195749674664)
XLA Ops:
  0.0 31.9 %shard_map.118 = bf16[8,128,256]{2,1,0:T(8,128)(2,1)S(1)} custom-call(bf16[8,128,256]{2,1,0:T(8,128)(2,1)} %bitcast.12, s32[1,256]{1,0:T(1,128)} %face_rows.1, s32[6,8,1,128]{3,2,1,0:T(1,128)} %bitcast.13, s32[1,64]{1,0:T(1,128)} %block_len.1, s32[1,4,8]{2,1,0:T(4,128)} %bitcast.14, s32[1,8,8]{2,1,0:T(8,128)} %pick.1, bf16[1792,256]{1,0:T(8,128)(2,1)} %bitcast.11, ...), custom_call_target="tpu_custom_call" | custom-call | tf_op jit(solution)/shard_map/pallas_call | solution.py:425
  31.9 0.8 %copy.14 = bf16[1,1024,256]{2,1,0:T(8,128)(2,1)} copy(bf16[1,1024,256]{2,1,0:T(8,128)(2,1)S(1)} %bitcast.10) | data formatting | bytes 1048576
